TPU v7x, 512 devices: a whole 4x8x8 slice. The times are simulated.
512 devices in a mesh: ta: 16 (over y, core), sa: 32 (over x, z).
Axes of the slice: x: 4, y: 8, z: 8, core: 2. Of those that a mesh axis runs over, the one named last changes fastest.
Arguments:
- gauge_links: float32 [4, 2, 3, 3, 32, 128, 128], P(None, None, None, None, 'sa', 'ta'), as said below
- noise_field: float32 [4, 8, 32, 128, 128], P(None, None, 'sa', 'ta'), may hold values from -6 to 6
Outputs:
- cooled_links: float32 [4, 2, 3, 3, 32, 128, 128], P(None, None, None, None, 'sa', 'ta')
- unitarity_norms: float32 [3, 128], P(None, 'ta')
Inputs may be any that keep to these rules, and one draw needn't show every extreme that they name: `gauge_links`: every link matrix has determinant one.
All inputs are finite; a program needn't handle non-finite values.
Results may differ from a plain program's by a relative error of at most 0.0003.
Values sent between devices are 32-bit elements; how exact they have to be, the bound alone decides.
A program may use at most 192 MiB of HBM per device.

v0:
```python
import functools
import math

import jax
import jax.numpy as jnp
from jax import lax
from jax.experimental import pallas as pl
from jax.experimental.pallas import tpu as pltpu
from jax.sharding import PartitionSpec as P

NY = 8
NZ = 16
LANES = NY * NZ
ROWS = 8

COUPLING = 5.6
STEP_SIZE = 0.02
COOL_SIZE = 0.02
FUGACITY = 0.5
ANTI_FUGACITY = 0.02

MESH = pl.DeviceIdType.MESH
TILE = (ROWS, LANES)
MAT = (2, 3, 3) + TILE
HERM = (9,) + TILE


def load(ref):
    return (ref[0], ref[1])


def store(ref, m):
    ref[0] = m[0]
    ref[1] = m[1]


def add(a, b):
    return (a[0] + b[0], a[1] + b[1])


def sub(a, b):
    return (a[0] - b[0], a[1] - b[1])


def mm(a, b):
    ar, ai = a
    br, bi = b
    re = im = None
    for k in range(3):
        cr, ci = ar[:, k : k + 1], ai[:, k : k + 1]
        rr, ri = br[k : k + 1], bi[k : k + 1]
        tr = cr * rr - ci * ri
        ti = cr * ri + ci * rr
        re = tr if re is None else re + tr
        im = ti if im is None else im + ti
    return (re, im)


def roll_rows(x, n):
    return jnp.concatenate([x[n:], x[:n]], axis=0)


def roll_cols(x, n):
    return jnp.concatenate([x[:, n:], x[:, :n]], axis=1)


def transposed(x):
    return jnp.stack([x[:, i] for i in range(3)])


def cmul(a, b):
    return (a[0] * b[0] - a[1] * b[1], a[0] * b[1] + a[1] * b[0])


def adj(m):
    one = tuple(roll_rows(x, 1) for x in m)
    two = tuple(roll_rows(x, 2) for x in m)
    plus = cmul(tuple(roll_cols(x, 1) for x in one), tuple(roll_cols(x, 2) for x in two))
    minus = cmul(tuple(roll_cols(x, 2) for x in one), tuple(roll_cols(x, 1) for x in two))
    return (transposed(plus[0] - minus[0]), transposed(plus[1] - minus[1]))


def less_inverse(p):
    return sub(p, adj(p))


def entry(m, i, j):
    return (m[0][i, j], m[1][i, j])


def add_diagonal(x, value):
    rows = []
    for i in range(3):
        parts = [(x[i, i] + value)[None]]
        if i > 0:
            parts.insert(0, x[i, :i])
        if i < 2:
            parts.append(x[i, i + 1 :])
        rows.append(jnp.concatenate(parts, axis=0))
    return jnp.stack(rows)


def inverse(m):
    a = adj(m)
    det = cmul(entry(m, 0, 0), entry(a, 0, 0))
    for j in (1, 2):
        det = add(det, cmul(entry(m, 0, j), entry(a, j, 0)))
    scale = 1.0 / (det[0] * det[0] + det[1] * det[1])
    factor = ((det[0] * scale)[None, None], (-det[1] * scale)[None, None])
    return cmul(a, factor)


def exp_times(y, u):
    square = mm(y, y)
    trace = tuple(x[0, 0] + x[1, 1] + x[2, 2] for x in square)
    det = None
    for j in range(3):
        a, b = (j + 1) % 3, (j + 2) % 3
        minor = sub(
            cmul(entry(y, 1, a), entry(y, 2, b)), cmul(entry(y, 1, b), entry(y, 2, a))
        )
        term = cmul(entry(y, 0, j), minor)
        det = term if det is None else add(det, term)
    beta = ((1.0 + trace[0] * (1.0 / 12.0))[None, None], (trace[1] * (1.0 / 12.0))[None, None])
    linear = cmul(y, beta)
    re = add_diagonal(linear[0] + 0.5 * square[0], 1.0 + det[0] * (1.0 / 6.0))
    im = add_diagonal(linear[1] + 0.5 * square[1], det[1] * (1.0 / 6.0))
    return mm((re, im), u)


def gram_rows(m):
    re, im = m
    diag = re * re + im * im
    a = tuple(jnp.concatenate([x[0:1], x[0:1], x[1:2]], axis=0) for x in m)
    b = tuple(jnp.concatenate([x[1:2], x[2:3], x[2:3]], axis=0) for x in m)
    pr = a[0] * b[0] + a[1] * b[1]
    pi = a[1] * b[0] - a[0] * b[1]
    return tuple(x[:, 0] + x[:, 1] + x[:, 2] for x in (diag, pr, pi))


def gram_cols(m):
    re, im = m
    diag = re * re + im * im
    a = tuple(jnp.concatenate([x[:, 0:1], x[:, 0:1], x[:, 1:2]], axis=1) for x in m)
    b = tuple(jnp.concatenate([x[:, 1:2], x[:, 2:3], x[:, 2:3]], axis=1) for x in m)
    pr = a[0] * b[0] + a[1] * b[1]
    pi = a[0] * b[1] - a[1] * b[0]
    return tuple(x[0] + x[1] + x[2] for x in (diag, pr, pi))


def h_add(a, b):
    return tuple(x + y for x, y in zip(a, b))


def h_sub(a, b):
    return tuple(x - y for x, y in zip(a, b))


def h_pack(h):
    return jnp.concatenate(h, axis=0)


def h_unpack(x):
    return (x[0:3], x[3:6], x[6:9])


def h_offsets(h):
    _, r, i = h
    one = (jnp.stack([r[0], r[2], r[1]]), jnp.stack([i[0], i[2], -i[1]]))
    two = (jnp.stack([r[1], r[0], r[2]]), jnp.stack([i[1], -i[0], -i[2]]))
    return one, two


def h_times(h, m):
    d = h[0][:, None]
    one, two = h_offsets(h)
    re, im = d * m[0], d * m[1]
    for n, off in ((1, one), (2, two)):
        r, i = off[0][:, None], off[1][:, None]
        ur, ui = roll_rows(m[0], n), roll_rows(m[1], n)
        re = re + r * ur - i * ui
        im = im + r * ui + i * ur
    return (re, im)


def times_h(m, h):
    d = h[0][None]
    one, two = h_offsets(h)
    re, im = m[0] * d, m[1] * d
    for n, off in ((1, one), (2, two)):
        r, i = off[0][None], off[1][None]
        ur, ui = roll_cols(m[0], n), roll_cols(m[1], n)
        re = re + ur * r + ui * i
        im = im + ui * r - ur * i
    return (re, im)


def h_full(h):
    d, r, i = h
    zero = jnp.zeros_like(d[0])
    re = jnp.stack(
        [jnp.stack([d[0], r[0], r[1]]), jnp.stack([r[0], d[1], r[2]]), jnp.stack([r[1], r[2], d[2]])]
    )
    im = jnp.stack(
        [jnp.stack([zero, i[0], i[1]]), jnp.stack([-i[0], zero, i[2]]), jnp.stack([-i[1], -i[2], zero])]
    )
    return (re, im)


def h_sandwich(h, s):
    m = times_h(h_times(h, h_full(s)), h)
    return (
        jnp.stack([m[0][0, 0], m[0][1, 1], m[0][2, 2]]),
        jnp.stack([m[0][0, 1], m[0][0, 2], m[0][1, 2]]),
        jnp.stack([m[1][0, 1], m[1][0, 2], m[1][1, 2]]),
    )


def cooling_pair(g):
    third = (g[0][0] + g[0][1] + g[0][2]) * (1.0 / 3.0)
    d = g[0] - third[None]
    p, q, r = ((g[1][n], g[2][n]) for n in range(3))
    norms = g[1] * g[1] + g[2] * g[2]
    np_, nq, nr = norms[0], norms[1], norms[2]
    d0, d1, d2 = d[0], d[1], d[2]
    s0 = d0 * d0 + np_ + nq
    s1 = d1 * d1 + np_ + nr
    s2 = d2 * d2 + nq + nr
    sp = (q[0] * r[0] + q[1] * r[1] - d2 * p[0], q[1] * r[0] - q[0] * r[1] - d2 * p[1])
    prod = cmul(p, r)
    sq = (prod[0] - d1 * q[0], prod[1] - d1 * q[1])
    sr = (p[0] * q[0] + p[1] * q[1] - d0 * r[0], p[0] * q[1] - p[1] * q[0] - d0 * r[1])
    half = 0.5 * (s0 + s1 + s2)
    det = (
        d0 * d1 * d2
        + 2.0 * (prod[0] * q[0] + prod[1] * q[1])
        - d0 * nr
        - d1 * nq
        - d2 * np_
    )
    a = COOL_SIZE
    linear = (a + (a**3 / 6.0) * half)[None]
    constant = ((a**3 / 6.0) * det)[None]
    even = (
        1.0 + (a * a / 2.0) * jnp.stack([s0, s1, s2]),
        (a * a / 2.0) * jnp.stack([sp[0], sq[0], sr[0]]),
        (a * a / 2.0) * jnp.stack([sp[1], sq[1], sr[1]]),
    )
    odd = (linear * d + constant, linear * g[1], linear * g[2])
    return h_sub(even, odd), h_add(even, odd)


def index_of(axis, ndim):
    return lax.broadcasted_iota(jnp.int32, (1,) * (ndim - 2) + TILE, ndim - 2 + axis)


def shift(x, direction, sign, halo=None):
    n = x.ndim
    if direction == 1:
        return pltpu.roll(x, LANES - NZ if sign > 0 else NZ, n - 1)
    if direction == 2:
        z = index_of(1, n) % NZ
        if sign > 0:
            return jnp.where(
                z == NZ - 1, pltpu.roll(x, NZ - 1, n - 1), pltpu.roll(x, LANES - 1, n - 1)
            )
        return jnp.where(z == 0, pltpu.roll(x, LANES - NZ + 1, n - 1), pltpu.roll(x, 1, n - 1))
    t = index_of(0, n)
    if sign > 0:
        return jnp.where(t == ROWS - 1, halo, pltpu.roll(x, ROWS - 1, n - 2))
    return jnp.where(t == 0, halo, pltpu.roll(x, 1, n - 2))


def m_shift(m, direction, sign, halo=(None, None)):
    return (shift(m[0], direction, sign, halo[0]), shift(m[1], direction, sign, halo[1]))


def h_shift(h, direction, sign, halo=None):
    return h_unpack(shift(h_pack(h), direction, sign, halo))


def unit_where(m, mask):
    one = jnp.where(mask, 1.0, 0.0)
    re = jnp.where(mask, 0.0, m[0])
    im = jnp.where(mask, 0.0, m[1])
    return (add_diagonal(re, one[0, 0]), im)


def time_scan(u, reverse):
    t = index_of(0, 4)
    for step in (1, 2, 4):
        if reverse:
            other = tuple(pltpu.roll(x, ROWS - step, 2) for x in u)
            u = mm(u, unit_where(other, t >= ROWS - step))
        else:
            other = tuple(pltpu.roll(x, step, 2) for x in u)
            u = mm(unit_where(other, t < step), u)
    return u


def kernel(
    sizes,
    u_hbm,
    noise_hbm,
    out_hbm,
    norm_ref,
    u,
    noise,
    inv,
    ahead_x,
    ahead_t,
    qx,
    qx_in,
    qt,
    qt_in,
    slab,
    slabs,
    acc,
    new,
    work,
    final,
    inner,
    inner_in,
    gauge,
    gauge_in,
    norm_tile,
    norm_inner,
    norm_part,
    norm_outer,
    local_sem,
    send_sem,
    recv_sem,
    slab_send,
    slab_recv,
    norm_send,
    norm_recv,
):
    n_ta, n_sa, n_in = sizes
    n_out = n_sa // n_in
    k, j = lax.axis_index("ta"), lax.axis_index("sa")
    j_out, j_in = j // n_in, j % n_in
    t_up, t_down = (lax.rem(k + 1, n_ta), j), (lax.rem(k + n_ta - 1, n_ta), j)
    x_up, x_down = (k, lax.rem(j + 1, n_sa)), (k, lax.rem(j + n_sa - 1, n_sa))
    around = [(lax.rem(k + n_ta - d, n_ta), j) for d in range(1, n_ta)]
    inner_at = [lax.rem(j_in + d, n_in) for d in range(1, n_in)]
    outer_at = [lax.rem(j_out + d, n_out) for d in range(1, n_out)]
    inner_group = [(k, j_out * n_in + at) for at in inner_at]
    outer_group = [(k, at * n_in + j_in) for at in outer_at]

    barrier = pltpu.get_barrier_semaphore()
    partners = around + [x_up, x_down] + inner_group + outer_group
    for device in partners:
        pl.semaphore_signal(barrier, inc=1, device_id=device, device_id_type=MESH)

    loads = [pltpu.make_async_copy(u_hbm.at[d], u.at[d], local_sem.at[d]) for d in range(4)]
    loads.append(pltpu.make_async_copy(noise_hbm, noise, local_sem.at[4]))
    for copy in loads:
        copy.start()

    started = []

    def send(src, dst, device):
        at = len(started)
        copy = pltpu.make_async_remote_copy(
            src_ref=src,
            dst_ref=dst,
            send_sem=send_sem.at[at],
            recv_sem=recv_sem.at[at],
            device_id=device,
            device_id_type=MESH,
        )
        copy.start()
        started.append(copy)
        return copy

    for copy in loads[:4]:
        copy.wait()
    links = [u.at[d] for d in range(4)]
    invs = [inv.at[d] for d in range(4)]
    for d in range(4):
        store(invs[d], adj(load(links[d])))

    def x_corner(nu, halo=(None, None)):
        middle = mm(load(invs[nu]), load(links[0]))
        return mm(m_shift(load(invs[0]), nu, 1, halo), middle)

    store(qx.at[0], x_corner(1))
    store(slab, time_scan(load(links[3]), True))

    pl.semaphore_wait(barrier, len(partners))

    got_ux = {}
    got_qx = {}
    got_ux[3] = send(u.at[3], ahead_x.at[2], x_down)
    got_qx[1] = send(qx.at[0], qx_in.at[0], x_up)
    got_ux[1] = send(u.at[1], ahead_x.at[0], x_down)
    got_ut = send(inv.at[0:3, :, :, :, 0:1, :], ahead_t.at[:, :, :, :, 0:1, :], t_down)
    slab_copies = []
    for d in range(1, n_ta):
        at = d - 1
        row = at // 2
        copy = pltpu.make_async_remote_copy(
            src_ref=slab.at[:, :, :, 0:1, :],
            dst_ref=slabs.at[at % 2, :, :, :, row : row + 1, :],
            send_sem=slab_send.at[at],
            recv_sem=slab_recv.at[at],
            device_id=around[at],
            device_id_type=MESH,
        )
        copy.start()
        slab_copies.append(copy)
    got_ux[2] = send(u.at[2], ahead_x.at[1], x_down)
    store(qx.at[1], x_corner(2))
    got_qx[2] = send(qx.at[1], qx_in.at[1], x_up)

    def t_corner(nu, ahead):
        return mm(mm(load(invs[3]), load(links[nu])), ahead)

    got_qt = {}
    for nu in (1, 2):
        store(qt.at[nu], t_corner(nu, m_shift(load(links[3]), nu, 1)))
    got_qt[1] = send(qt.at[1:3, :, :, :, 7:8, :], qt_in.at[1:3, :, :, :, 7:8, :], t_up)

    u_1, u_2 = load(links[1]), load(links[2])
    n_12 = mm(m_shift(u_2, 1, 1), m_shift(load(invs[1]), 2, 1))
    m_12 = mm(load(invs[2]), u_1)
    a_12 = less_inverse(mm(u_1, mm(n_12, load(invs[2]))))
    store(acc.at[1], sub(a_12, m_shift(less_inverse(mm(m_12, n_12)), 2, -1)))
    store(acc.at[2], sub(m_shift(less_inverse(mm(n_12, m_12)), 1, -1), a_12))

    got_ut.wait_recv()

    def inv_ahead(nu):
        return (ahead_t[nu, 0, :, :, 0:1, :], ahead_t[nu, 1, :, :, 0:1, :])

    store(qx.at[2], x_corner(3, inv_ahead(0)))
    got_qx[3] = send(qx.at[2], qx_in.at[2], x_up)

    def accumulate(d, term, sign):
        now = load(acc.at[d])
        store(acc.at[d], add(now, term) if sign > 0 else sub(now, term))

    got_qt[1].wait_recv()

    def behind_t(nu):
        return (qt_in[nu, 0, :, :, 7:8, :], qt_in[nu, 1, :, :, 7:8, :])

    for nu in (1, 2):
        n_nt = mm(m_shift(load(links[3]), nu, 1), m_shift(load(invs[nu]), 3, 1, inv_ahead(nu)))
        a_nt = less_inverse(mm(load(links[nu]), mm(n_nt, load(invs[3]))))
        m_nt = mm(load(invs[3]), load(links[nu]))
        lower = mm(m_shift(load(qt.at[nu]), 3, -1, behind_t(nu)), load(invs[nu]))
        accumulate(nu, sub(a_nt, less_inverse(lower)), 1)
        to_t = sub(m_shift(less_inverse(mm(n_nt, m_nt)), nu, -1), a_nt)
        if nu == 1:
            store(acc.at[3], to_t)
        else:
            accumulate(3, to_t, 1)

    got_ux[3].wait_recv()
    store(qt.at[0], t_corner(0, load(ahead_x.at[2])))
    got_qt[0] = send(qt.at[0, :, :, :, 7:8, :], qt_in.at[0, :, :, :, 7:8, :], t_up)

    prefix = time_scan(load(links[3]), False)
    first = index_of(0, 4) == 0
    prefix = unit_where(tuple(pltpu.roll(x, 1, 2) for x in prefix), first)
    for copy in slab_copies:
        copy.wait_recv()
    slot = 2 * index_of(0, 4)
    even, odd = load(slabs.at[0]), load(slabs.at[1])
    if n_ta - 1 < 2 * ROWS - 1:
        even = unit_where(even, slot >= n_ta - 1)
    odd = unit_where(odd, slot + 1 >= n_ta - 1)
    others = mm(even, odd)
    for step in (1, 2, 4):
        others = mm(others, tuple(pltpu.roll(x, ROWS - step, 2) for x in others))
    others = tuple(jnp.broadcast_to(x[:, :, 0:1, :], x.shape) for x in others)
    line = mm(mm(load(slab), others), prefix)
    back = adj(line)
    former = (add_diagonal(FUGACITY * line[0], 1.0), FUGACITY * line[1])
    latter = (add_diagonal(ANTI_FUGACITY * back[0], 1.0), ANTI_FUGACITY * back[1])
    drift = sub(inverse(latter), inverse(former))
    weight = 4.0 * 3.0 / COUPLING
    accumulate(3, (weight * drift[0], weight * drift[1]), 1)

    for nu in (3, 1, 2):
        if nu != 3:
            got_ux[nu].wait_recv()
        halo = inv_ahead(0) if nu == 3 else (None, None)
        n_xn = mm(load(ahead_x.at[nu - 1]), m_shift(load(invs[0]), nu, 1, halo))
        a_xn = less_inverse(mm(load(links[0]), mm(n_xn, load(invs[nu]))))
        if nu == 3:
            store(acc.at[0], a_xn)
        else:
            m_xn = mm(load(invs[nu]), load(links[0]))
            lower = m_shift(less_inverse(mm(m_xn, n_xn)), nu, -1)
            accumulate(0, sub(a_xn, lower), 1)
        accumulate(nu, a_xn, -1)

    got_qt[0].wait_recv()
    lower = mm(m_shift(load(qt.at[0]), 3, -1, behind_t(0)), load(invs[0]))
    accumulate(0, less_inverse(lower), -1)

    loads[4].wait()
    c = math.sqrt(STEP_SIZE)

    def update(d):
        x = load(acc.at[d])
        w = -STEP_SIZE * COUPLING / 3.0
        mean_r = (x[0][0, 0] + x[0][1, 1] + x[0][2, 2]) * (1.0 / 3.0)
        mean_i = (x[1][0, 0] + x[1][1, 1] + x[1][2, 2]) * (1.0 / 3.0)
        n = [c * noise[d, a] for a in range(8)]
        n7 = n[7] * (1.0 / math.sqrt(3.0))
        real = {(0, 1): n[1], (0, 2): n[4], (1, 2): n[6]}
        imag = {(0, 1): n[0], (0, 2): n[3], (1, 2): n[5]}
        diag = (n[2] + n7, n7 - n[2], -2.0 * n7)
        yr, yi = [], []
        for a in range(3):
            row_r, row_i = [], []
            for b in range(3):
                if a == b:
                    row_r.append(w * (x[0][a, b] - mean_r))
                    row_i.append(w * (x[1][a, b] - mean_i) + diag[a])
                elif a < b:
                    row_r.append(w * x[0][a, b] + real[a, b])
                    row_i.append(w * x[1][a, b] + imag[a, b])
                else:
                    row_r.append(w * x[0][a, b] - real[b, a])
                    row_i.append(w * x[1][a, b] + imag[b, a])
            yr.append(jnp.stack(row_r))
            yi.append(jnp.stack(row_i))
        m = exp_times((jnp.stack(yr), jnp.stack(yi)), load(links[d]))
        store(new.at[d], m)
        return m

    m = update(0)
    inner[0] = h_pack(gram_cols(m))
    got_inner_x = send(inner.at[0], inner_in.at[0], x_up)
    plus = gram_rows(m)
    for nu in (1, 2, 3):
        got_qx[nu].wait_recv()
        accumulate(nu, less_inverse(mm(load(links[nu]), load(qx_in.at[nu - 1]))), 1)
        if nu == 3:
            m = update(3)
            inner[1] = h_pack(gram_cols(m))
            got_inner_t = send(inner.at[1, :, 7:8, :], inner_in.at[1, :, 7:8, :], t_up)
            plus = h_add(plus, gram_rows(m))
    minus = None
    for d in (1, 2):
        m = update(d)
        plus = h_add(plus, gram_rows(m))
        lagged = h_shift(gram_cols(m), d, -1)
        minus = lagged if minus is None else h_add(minus, lagged)
    norms = [plus[0][0] + plus[0][1] + plus[0][2]]
    got_inner_t.wait_recv()
    minus = h_add(minus, h_unpack(shift(inner[1], 3, -1, inner_in[1, :, 7:8, :])))
    got_inner_x.wait_recv()
    minus = h_add(minus, h_unpack(inner_in[0]))

    low, high = cooling_pair(h_sub(plus, minus))
    gauge[0] = h_pack(high)
    got_high_x = send(gauge.at[0], gauge_in.at[0], x_down)
    got_high_t = send(gauge.at[0, :, 0:1, :], gauge_in.at[1, :, 0:1, :], t_down)

    m = h_times(low, load(new.at[0]))
    store(work.at[0], m)
    inner[2] = h_pack(gram_cols(m))
    got_inner_x = send(inner.at[2], inner_in.at[2], x_up)
    m = h_times(low, load(new.at[3]))
    store(work.at[3], m)
    inner[3] = h_pack(gram_cols(m))
    got_inner_t = send(inner.at[3, :, 7:8, :], inner_in.at[3, :, 7:8, :], t_up)
    plus = minus = None
    for d in (1, 2):
        m = h_times(low, load(new.at[d]))
        lagged = h_shift(gram_cols(m), d, -1)
        minus = lagged if minus is None else h_add(minus, lagged)
        m = times_h(m, h_shift(high, d, 1))
        store(new.at[d], m)
        plus = gram_rows(m) if plus is None else h_add(plus, gram_rows(m))
    got_high_t.wait_recv()
    m = times_h(load(work.at[3]), h_unpack(shift(gauge[0], 3, 1, gauge_in[1, :, 0:1, :])))
    store(new.at[3], m)
    plus = h_add(plus, gram_rows(m))
    got_inner_t.wait_recv()
    minus = h_add(minus, h_unpack(shift(inner[3], 3, -1, inner_in[3, :, 7:8, :])))
    got_high_x.wait_recv()
    m = times_h(load(work.at[0]), h_unpack(gauge_in[0]))
    store(new.at[0], m)
    plus = h_add(plus, gram_rows(m))
    norms.append(plus[0][0] + plus[0][1] + plus[0][2])
    got_inner_x.wait_recv()
    minus = h_add(minus, h_unpack(inner_in[2]))
    minus = h_sandwich(h_unpack(gauge[0]), minus)

    low, high = cooling_pair(h_sub(plus, minus))
    gauge[1] = h_pack(high)
    got_high_x = send(gauge.at[1], gauge_in.at[2], x_down)
    got_high_t = send(gauge.at[1, :, 0:1, :], gauge_in.at[3, :, 0:1, :], t_down)
    total = None
    writes = []

    def finish(d, m, total):
        store(final.at[d], m)
        copy = pltpu.make_async_copy(final.at[d], out_hbm.at[d], local_sem.at[d])
        copy.start()
        writes.append(copy)
        squares = m[0] * m[0] + m[1] * m[1]
        squares = squares[0] + squares[1] + squares[2]
        squares = squares[0] + squares[1] + squares[2]
        return squares if total is None else total + squares

    for d in (1, 2):
        m = times_h(h_times(low, load(new.at[d])), h_shift(high, d, 1))
        total = finish(d, m, total)
    last_t = h_times(low, load(new.at[3]))
    store(work.at[0], h_times(low, load(new.at[0])))
    got_high_t.wait_recv()
    m = times_h(last_t, h_unpack(shift(gauge[1], 3, 1, gauge_in[3, :, 0:1, :])))
    total = finish(3, m, total)
    got_high_x.wait_recv()
    total = finish(0, times_h(load(work.at[0]), h_unpack(gauge_in[2])), total)
    norms.append(total)

    row, lane = index_of(0, 2), index_of(1, 2)
    tile = jnp.zeros(TILE, jnp.float32)
    for at, value in enumerate(norms):
        sums = jnp.sum(value, axis=1, keepdims=True)
        as_row = jnp.sum(jnp.where(row == lane, sums, 0.0), axis=0, keepdims=True)
        tile = jnp.where(row == at, as_row, tile)

    def summed(tile, src, buffer, mine, others_at, group, sem0):
        src[...] = tile
        buffer[mine] = tile
        copies = []
        for d, device in enumerate(group):
            copy = pltpu.make_async_remote_copy(
                src_ref=src,
                dst_ref=buffer.at[mine],
                send_sem=norm_send.at[sem0 + d],
                recv_sem=norm_recv.at[sem0 + mine],
                device_id=device,
                device_id_type=MESH,
            )
            copy.start()
            copies.append(copy)
        for d, device in enumerate(group):
            pltpu.make_async_remote_copy(
                src_ref=src,
                dst_ref=buffer.at[others_at[d]],
                send_sem=norm_send.at[sem0 + d],
                recv_sem=norm_recv.at[sem0 + others_at[d]],
                device_id=device,
                device_id_type=MESH,
            ).wait_recv()
        result = buffer[0]
        for at in range(1, len(group) + 1):
            result = result + buffer[at]
        return result, copies

    tile, copies = summed(tile, norm_tile, norm_inner, j_in, inner_at, inner_group, 0)
    started.extend(copies)
    tile, copies = summed(tile, norm_part, norm_outer, j_out, outer_at, outer_group, n_in)
    started.extend(copies)
    site_count = n_sa * LANES
    norm_ref[...] = tile[0:3, 0:ROWS] * (1.0 / (4.0 * site_count)) - 3.0

    for copy in started + slab_copies:
        copy.wait_send()
    for copy in writes:
        copy.wait()


def local(gauge_links, noise_field):
    n_ta, n_sa = lax.axis_size("ta"), lax.axis_size("sa")
    n_in = max(n_sa // 4, 2)
    n_out = n_sa // n_in
    shape = (4,) + MAT
    vmem = lambda *s: pltpu.VMEM(s, jnp.float32)
    dma = lambda n: pltpu.SemaphoreType.DMA((n,))
    cooled, norms = pl.pallas_call(
        functools.partial(kernel, (n_ta, n_sa, n_in)),
        out_shape=(
            jax.ShapeDtypeStruct(shape, jnp.float32),
            jax.ShapeDtypeStruct((3, ROWS), jnp.float32),
        ),
        in_specs=[pl.BlockSpec(memory_space=pl.ANY)] * 2,
        out_specs=(
            pl.BlockSpec(memory_space=pl.ANY),
            pl.BlockSpec(memory_space=pltpu.VMEM),
        ),
        scratch_shapes=[
            vmem(*shape),
            vmem(4, 8, *TILE),
            vmem(*shape),
            vmem(3, *MAT),
            vmem(3, *MAT),
            vmem(3, *MAT),
            vmem(3, *MAT),
            vmem(3, *MAT),
            vmem(3, *MAT),
            vmem(*MAT),
            vmem(2, *MAT),
            vmem(*shape),
            vmem(*shape),
            vmem(*shape),
            vmem(*shape),
            vmem(4, *HERM),
            vmem(4, *HERM),
            vmem(2, *HERM),
            vmem(4, *HERM),
            vmem(*TILE),
            vmem(n_in, *TILE),
            vmem(*TILE),
            vmem(n_out, *TILE),
            dma(5),
            dma(24),
            dma(24),
            dma(n_ta - 1),
            dma(n_ta - 1),
            dma(n_in + n_out),
            dma(n_in + n_out),
        ],
        compiler_params=pltpu.CompilerParams(
            collective_id=0, has_side_effects=True, vmem_limit_bytes=32 * 1024 * 1024
        ),
        name="langevin_step",
    )(gauge_links.reshape(shape), noise_field.reshape((4, 8) + TILE))
    return cooled.reshape(gauge_links.shape), norms


def solution(mesh):
    placed = (P(None, None, None, None, "sa", "ta", None), P(None, None, "sa", "ta", None))
    return jax.shard_map(
        local,
        mesh=mesh,
        in_specs=placed,
        out_specs=(P(None, None, None, None, "sa", "ta", None), P(None, "ta")),
        check_vma=False,
    )
```

profile of v0, /device:TPU:2, one launch (start us, length us, event | category | flops | bytes accessed | tf_op | source)
XLA Modules:
  0.0 46.5 jit_solution(11016996425610406157)
XLA Ops:
  0.6 0.0 copy-start
  0.6 1.0 %copy-done = f32[4,2,3,3,1,8,128]{6,5,4,3,2,1,0:T(8,128)S(1)} copy-done((f32[4,2,3,3,1,8,128]{6,5,4,3,2,1,0:T(8,128)S(1)}, f32[4,2,3,3,1,8,128]{6,5,4,3,2,1,0:T(8,128)}, u32[]{:S(2)}) %copy-start) | copy-done | bytes 294936
  1.6 0.0 copy-start.1
  1.6 0.9 %copy-done.1 = f32[4,8,1,8,128]{4,3,2,1,0:T(8,128)S(1)} copy-done((f32[4,8,1,8,128]{4,3,2,1,0:T(8,128)S(1)}, f32[4,8,1,8,128]{4,3,2,1,0:T(8,128)}, u32[]{:S(2)}) %copy-start.1) | copy-done | bytes 131096
  2.5 42.7 %langevin_step.1 = (f32[4,2,3,3,8,128]{5,4,3,2,1,0:T(8,128)S(1)}, f32[3,8]{1,0:T(4,128)S(1)}) custom-call(f32[4,2,3,3,8,128]{5,4,3,2,1,0:T(8,128)S(1)} %bitcast.6, f32[4,8,8,128]{3,2,1,0:T(8,128)S(1)} %bitcast.7), custom_call_target="tpu_custom_call" | custom-call | tf_op jit(solution)/shard_map/langevin_step/pallas_call | solution.py:681
  45.2 0.7 %copy.7 = f32[4,2,3,3,1,8,128]{6,5,4,3,2,1,0:T(8,128)} copy(f32[4,2,3,3,1,8,128]{6,5,4,3,2,1,0:T(8,128)S(1)} %bitcast.5) | data formatting | bytes 589824
  45.9 0.6 %copy.8 = f32[3,8]{1,0:T(4,128)} copy(f32[3,8]{1,0:T(4,128)S(1)} %get-tuple-element.11) | data formatting | bytes 192
Async XLA Ops:
  0.6 1.0 %copy-start = (f32[4,2,3,3,1,8,128]{6,5,4,3,2,1,0:T(8,128)S(1)}, f32[4,2,3,3,1,8,128]{6,5,4,3,2,1,0:T(8,128)}, u32[]{:S(2)}) copy-start(f32[4,2,3,3,1,8,128]{6,5,4,3,2,1,0:T(8,128)} %param.2) | copy-start | bytes 884740
  1.6 0.9 %copy-start.1 = (f32[4,8,1,8,128]{4,3,2,1,0:T(8,128)S(1)}, f32[4,8,1,8,128]{4,3,2,1,0:T(8,128)}, u32[]{:S(2)}) copy-start(f32[4,8,1,8,128]{4,3,2,1,0:T(8,128)} %param.3) | copy-start | bytes 393220
where the time goes:
time: 46.7 us; the launch traced here: 46.5 us
  Pallas kernels  42.7 us (91%)
  local copies, waits for them, and re-layouts  3.15 us (7%)
  between operations  0.65 us (1%)
    pallas_call x1, Pallas kernels, local(): pl.pallas_call(functools.partial(kernel, (n_ta, n_sa, n_in)), out_shape=(...  42.7 us
    unnamed x6, local copies, waits for them, and re-layouts  3.15 us

commit v1 on v0

v1 whole, which is shorter than its diff:
```python
import functools
import math

import jax
import jax.numpy as jnp
from jax import lax
from jax.experimental import pallas as pl
from jax.experimental.pallas import tpu as pltpu
from jax.sharding import PartitionSpec as P

NY = 8
NZ = 16
LANES = NY * NZ
ROWS = 8

COUPLING = 5.6
STEP_SIZE = 0.02
COOL_SIZE = 0.02
FUGACITY = 0.5
ANTI_FUGACITY = 0.02

MESH = pl.DeviceIdType.MESH
VMEM_LIMIT = 32 * 1024 * 1024
TILE = (ROWS, LANES)
MATRIX = (3, 3) + TILE
MAT = 18
HERM = 9


def load(ref):
    return (ref[0:9].reshape(MATRIX), ref[9:18].reshape(MATRIX))


def load_row(ref, row):
    shape = (3, 3, 1, LANES)
    return tuple(ref[9 * c : 9 * c + 9, row : row + 1, :].reshape(shape) for c in range(2))


def store(ref, m):
    ref[0:9] = m[0].reshape((9,) + TILE)
    ref[9:18] = m[1].reshape((9,) + TILE)


def matrix_at(ref, at):
    return ref.at[MAT * at : MAT * (at + 1)]


def herm_at(ref, at):
    return ref.at[HERM * at : HERM * (at + 1)]


def row_of(ref, row):
    return ref.at[:, row : row + 1, :]


def add(a, b):
    return (a[0] + b[0], a[1] + b[1])


def sub(a, b):
    return (a[0] - b[0], a[1] - b[1])


def mm(a, b):
    ar, ai = a
    br, bi = b
    re = im = None
    for k in range(3):
        cr, ci = ar[:, k : k + 1], ai[:, k : k + 1]
        rr, ri = br[k : k + 1], bi[k : k + 1]
        tr = cr * rr - ci * ri
        ti = cr * ri + ci * rr
        re = tr if re is None else re + tr
        im = ti if im is None else im + ti
    return (re, im)


def roll_rows(x, n):
    return jnp.concatenate([x[n:], x[:n]], axis=0)


def roll_cols(x, n):
    return jnp.concatenate([x[:, n:], x[:, :n]], axis=1)


def transposed(x):
    return jnp.stack([x[:, i] for i in range(3)])


def cmul(a, b):
    return (a[0] * b[0] - a[1] * b[1], a[0] * b[1] + a[1] * b[0])


def adj(m):
    one = tuple(roll_rows(x, 1) for x in m)
    two = tuple(roll_rows(x, 2) for x in m)
    plus = cmul(tuple(roll_cols(x, 1) for x in one), tuple(roll_cols(x, 2) for x in two))
    minus = cmul(tuple(roll_cols(x, 2) for x in one), tuple(roll_cols(x, 1) for x in two))
    return (transposed(plus[0] - minus[0]), transposed(plus[1] - minus[1]))


def less_inverse(p):
    return sub(p, adj(p))


def entry(m, i, j):
    return (m[0][i, j], m[1][i, j])


def add_diagonal(x, value):
    rows = []
    for i in range(3):
        parts = [(x[i, i] + value)[None]]
        if i > 0:
            parts.insert(0, x[i, :i])
        if i < 2:
            parts.append(x[i, i + 1 :])
        rows.append(jnp.concatenate(parts, axis=0))
    return jnp.stack(rows)


def inverse(m):
    a = adj(m)
    det = cmul(entry(m, 0, 0), entry(a, 0, 0))
    for j in (1, 2):
        det = add(det, cmul(entry(m, 0, j), entry(a, j, 0)))
    scale = 1.0 / (det[0] * det[0] + det[1] * det[1])
    factor = ((det[0] * scale)[None, None], (-det[1] * scale)[None, None])
    return cmul(a, factor)


def exp_times(y, u):
    square = mm(y, y)
    trace = tuple(x[0, 0] + x[1, 1] + x[2, 2] for x in square)
    det = None
    for j in range(3):
        a, b = (j + 1) % 3, (j + 2) % 3
        minor = sub(
            cmul(entry(y, 1, a), entry(y, 2, b)), cmul(entry(y, 1, b), entry(y, 2, a))
        )
        term = cmul(entry(y, 0, j), minor)
        det = term if det is None else add(det, term)
    beta = ((1.0 + trace[0] * (1.0 / 12.0))[None, None], (trace[1] * (1.0 / 12.0))[None, None])
    linear = cmul(y, beta)
    re = add_diagonal(linear[0] + 0.5 * square[0], 1.0 + det[0] * (1.0 / 6.0))
    im = add_diagonal(linear[1] + 0.5 * square[1], det[1] * (1.0 / 6.0))
    return mm((re, im), u)


def gram_rows(m):
    re, im = m
    diag = re * re + im * im
    a = tuple(jnp.concatenate([x[0:1], x[0:1], x[1:2]], axis=0) for x in m)
    b = tuple(jnp.concatenate([x[1:2], x[2:3], x[2:3]], axis=0) for x in m)
    pr = a[0] * b[0] + a[1] * b[1]
    pi = a[1] * b[0] - a[0] * b[1]
    return tuple(x[:, 0] + x[:, 1] + x[:, 2] for x in (diag, pr, pi))


def gram_cols(m):
    re, im = m
    diag = re * re + im * im
    a = tuple(jnp.concatenate([x[:, 0:1], x[:, 0:1], x[:, 1:2]], axis=1) for x in m)
    b = tuple(jnp.concatenate([x[:, 1:2], x[:, 2:3], x[:, 2:3]], axis=1) for x in m)
    pr = a[0] * b[0] + a[1] * b[1]
    pi = a[0] * b[1] - a[1] * b[0]
    return tuple(x[0] + x[1] + x[2] for x in (diag, pr, pi))


def h_add(a, b):
    return tuple(x + y for x, y in zip(a, b))


def h_sub(a, b):
    return tuple(x - y for x, y in zip(a, b))


def h_pack(h):
    return jnp.concatenate(h, axis=0)


def h_unpack(x):
    return (x[0:3], x[3:6], x[6:9])


def h_offsets(h):
    _, r, i = h
    one = (jnp.stack([r[0], r[2], r[1]]), jnp.stack([i[0], i[2], -i[1]]))
    two = (jnp.stack([r[1], r[0], r[2]]), jnp.stack([i[1], -i[0], -i[2]]))
    return one, two


def h_times(h, m):
    d = h[0][:, None]
    one, two = h_offsets(h)
    re, im = d * m[0], d * m[1]
    for n, off in ((1, one), (2, two)):
        r, i = off[0][:, None], off[1][:, None]
        ur, ui = roll_rows(m[0], n), roll_rows(m[1], n)
        re = re + r * ur - i * ui
        im = im + r * ui + i * ur
    return (re, im)


def times_h(m, h):
    d = h[0][None]
    one, two = h_offsets(h)
    re, im = m[0] * d, m[1] * d
    for n, off in ((1, one), (2, two)):
        r, i = off[0][None], off[1][None]
        ur, ui = roll_cols(m[0], n), roll_cols(m[1], n)
        re = re + ur * r + ui * i
        im = im + ui * r - ur * i
    return (re, im)


def h_full(h):
    d, r, i = h
    zero = jnp.zeros_like(d[0])
    re = jnp.stack(
        [jnp.stack([d[0], r[0], r[1]]), jnp.stack([r[0], d[1], r[2]]), jnp.stack([r[1], r[2], d[2]])]
    )
    im = jnp.stack(
        [jnp.stack([zero, i[0], i[1]]), jnp.stack([-i[0], zero, i[2]]), jnp.stack([-i[1], -i[2], zero])]
    )
    return (re, im)


def h_sandwich(h, s):
    m = times_h(h_times(h, h_full(s)), h)
    return (
        jnp.stack([m[0][0, 0], m[0][1, 1], m[0][2, 2]]),
        jnp.stack([m[0][0, 1], m[0][0, 2], m[0][1, 2]]),
        jnp.stack([m[1][0, 1], m[1][0, 2], m[1][1, 2]]),
    )


def cooling_pair(g):
    third = (g[0][0] + g[0][1] + g[0][2]) * (1.0 / 3.0)
    d = g[0] - third[None]
    p, q, r = ((g[1][n], g[2][n]) for n in range(3))
    norms = g[1] * g[1] + g[2] * g[2]
    np_, nq, nr = norms[0], norms[1], norms[2]
    d0, d1, d2 = d[0], d[1], d[2]
    s0 = d0 * d0 + np_ + nq
    s1 = d1 * d1 + np_ + nr
    s2 = d2 * d2 + nq + nr
    sp = (q[0] * r[0] + q[1] * r[1] - d2 * p[0], q[1] * r[0] - q[0] * r[1] - d2 * p[1])
    prod = cmul(p, r)
    sq = (prod[0] - d1 * q[0], prod[1] - d1 * q[1])
    sr = (p[0] * q[0] + p[1] * q[1] - d0 * r[0], p[0] * q[1] - p[1] * q[0] - d0 * r[1])
    half = 0.5 * (s0 + s1 + s2)
    det = (
        d0 * d1 * d2
        + 2.0 * (prod[0] * q[0] + prod[1] * q[1])
        - d0 * nr
        - d1 * nq
        - d2 * np_
    )
    a = COOL_SIZE
    linear = (a + (a**3 / 6.0) * half)[None]
    constant = ((a**3 / 6.0) * det)[None]
    even = (
        1.0 + (a * a / 2.0) * jnp.stack([s0, s1, s2]),
        (a * a / 2.0) * jnp.stack([sp[0], sq[0], sr[0]]),
        (a * a / 2.0) * jnp.stack([sp[1], sq[1], sr[1]]),
    )
    odd = (linear * d + constant, linear * g[1], linear * g[2])
    return h_sub(even, odd), h_add(even, odd)


def index_of(axis, ndim):
    return lax.broadcasted_iota(jnp.int32, (1,) * (ndim - 2) + TILE, ndim - 2 + axis)


def shift(x, direction, sign, halo=None):
    n = x.ndim
    if direction == 1:
        return pltpu.roll(x, LANES - NZ if sign > 0 else NZ, n - 1)
    if direction == 2:
        z = index_of(1, n) % NZ
        if sign > 0:
            return jnp.where(
                z == NZ - 1, pltpu.roll(x, NZ - 1, n - 1), pltpu.roll(x, LANES - 1, n - 1)
            )
        return jnp.where(z == 0, pltpu.roll(x, LANES - NZ + 1, n - 1), pltpu.roll(x, 1, n - 1))
    t = index_of(0, n)
    if sign > 0:
        return jnp.where(t == ROWS - 1, halo, pltpu.roll(x, ROWS - 1, n - 2))
    return jnp.where(t == 0, halo, pltpu.roll(x, 1, n - 2))


def m_shift(m, direction, sign, halo=(None, None)):
    return (shift(m[0], direction, sign, halo[0]), shift(m[1], direction, sign, halo[1]))


def h_shift(h, direction, sign, halo=None):
    return h_unpack(shift(h_pack(h), direction, sign, halo))


def unit_where(m, mask):
    one = jnp.where(mask, 1.0, 0.0)
    re = jnp.where(mask, 0.0, m[0])
    im = jnp.where(mask, 0.0, m[1])
    return (add_diagonal(re, one[0, 0]), im)


def time_scan(u, reverse):
    t = index_of(0, 4)
    for step in (1, 2, 4):
        if reverse:
            other = tuple(pltpu.roll(x, ROWS - step, 2) for x in u)
            u = mm(u, unit_where(other, t >= ROWS - step))
        else:
            other = tuple(pltpu.roll(x, step, 2) for x in u)
            u = mm(unit_where(other, t < step), u)
    return u


def far_first(n_out, n_in):
    steps = [(a, b) for a in range(n_out) for b in range(n_in) if a or b]
    return sorted(steps, key=lambda s: -(min(s[0], n_out - s[0]) + min(s[1], n_in - s[1])))


def kernel(
    sizes,
    u_hbm,
    noise_hbm,
    out,
    norm_ref,
    u,
    noise,
    inv,
    ahead_x,
    ahead_t,
    ahead_xt,
    behind_xt,
    qx,
    qx_in,
    qt,
    qt_in,
    slab,
    slabs,
    prefix,
    acc,
    new,
    gx,
    gx_in,
    gt,
    gt_in,
    part,
    part_in,
    norm_row,
    norm_rows,
    local_sem,
    send_sem,
    recv_sem,
    slab_send,
    slab_recv,
    norm_send,
    norm_recv,
):
    n_ta, n_sa, n_in = sizes
    n_out = n_sa // n_in
    k, j = lax.axis_index("ta"), lax.axis_index("sa")
    j_out, j_in = j // n_in, j % n_in
    k_up, k_down = lax.rem(k + 1, n_ta), lax.rem(k + n_ta - 1, n_ta)
    j_up, j_down = lax.rem(j + 1, n_sa), lax.rem(j + n_sa - 1, n_sa)
    t_up, t_down, x_up, x_down = (k_up, j), (k_down, j), (k, j_up), (k, j_down)
    x_up_t_down, x_down_t_up = (k_down, j_up), (k_up, j_down)
    around = [lax.rem(k + n_ta - d, n_ta) for d in range(1, n_ta)]
    group = [
        lax.rem(j_out + a, n_out) * n_in + lax.rem(j_in + b, n_in)
        for a, b in far_first(n_out, n_in)
    ]

    barrier = pltpu.get_barrier_semaphore()
    partners = [
        (min(a, n_out - a) + min(b, n_in - b), (k, at))
        for (a, b), at in zip(far_first(n_out, n_in), group)
    ]
    partners += [(min(d, n_ta - d) / 2, (at, j)) for d, at in enumerate(around, 1)]
    partners += [(2.5, x_up_t_down), (2.5, x_down_t_up)]
    partners = [device for _, device in sorted(partners, key=lambda p: -p[0])]
    for device in partners:
        pl.semaphore_signal(barrier, inc=1, device_id=device, device_id_type=MESH)

    loads = [pltpu.make_async_copy(matrix_at(u_hbm, d), matrix_at(u, d), local_sem.at[d]) for d in range(4)]
    loads.append(pltpu.make_async_copy(noise_hbm, noise, local_sem.at[4]))
    for copy in loads:
        copy.start()

    started = []

    def send(src, dst, device):
        at = len(started)
        copy = pltpu.make_async_remote_copy(
            src_ref=src,
            dst_ref=dst,
            send_sem=send_sem.at[at],
            recv_sem=recv_sem.at[at],
            device_id=device,
            device_id_type=MESH,
        )
        copy.start()
        started.append(copy)
        return copy

    def accumulate(d, term, sign):
        now = load(matrix_at(acc, d))
        store(matrix_at(acc, d), add(now, term) if sign > 0 else sub(now, term))


    links = [matrix_at(u, d) for d in range(4)]
    invs = [matrix_at(inv, d) for d in range(4)]
    t_of = index_of(0, 4)
    for d in range(4):
        loads[d].wait()
        store(invs[d], adj(load(links[d])))

    for nu in (1, 2):
        middle = mm(load(invs[nu]), load(links[0]))
        store(matrix_at(qx, nu - 1), mm(m_shift(load(invs[0]), nu, 1), middle))
    middle = mm(load(invs[3]), load(links[0]))
    store(matrix_at(qt, 0), middle)
    raised = tuple(pltpu.roll(x, ROWS - 1, 2) for x in load(invs[0]))
    whole = mm(raised, middle)
    store(matrix_at(qx, 2), tuple(jnp.where(t_of == ROWS - 1, b, a) for a, b in zip(whole, middle)))

    for nu in (1, 2):
        store(matrix_at(qt, nu), mm(mm(load(invs[3]), load(links[nu])), m_shift(load(links[3]), nu, 1)))

    store(slab, time_scan(load(links[3]), True))
    scan = time_scan(load(links[3]), False)
    store(prefix, unit_where(tuple(pltpu.roll(x, 1, 2) for x in scan), t_of == 0))

    u_1, u_2 = load(links[1]), load(links[2])
    n_12 = mm(m_shift(u_2, 1, 1), m_shift(load(invs[1]), 2, 1))
    m_12 = mm(load(invs[2]), u_1)
    a_12 = less_inverse(mm(u_1, mm(n_12, load(invs[2]))))
    store(matrix_at(acc, 1), sub(a_12, m_shift(less_inverse(mm(m_12, n_12)), 2, -1)))
    store(matrix_at(acc, 2), sub(m_shift(less_inverse(mm(n_12, m_12)), 1, -1), a_12))


    pl.semaphore_wait(barrier, len(partners))

    got_ux, got_qx = {}, {}
    for nu in (3, 1, 2):
        got_ux[nu] = send(links[nu], matrix_at(ahead_x, nu - 1), x_down)
        got_qx[nu] = send(matrix_at(qx, nu - 1), matrix_at(qx_in, nu - 1), x_up)
    got_ut = send(inv.at[0 : 3 * MAT, 0:1, :], row_of(ahead_t, 0), t_down)
    got_qt = send(row_of(qt, 7), row_of(qt_in, 7), t_up)
    slab_copies = []
    far_order = sorted(range(1, n_ta), key=lambda d: -min(d, n_ta - d))
    for d in far_order:
        at = d - 1
        row = at // 2
        copy = pltpu.make_async_remote_copy(
            src_ref=row_of(slab, 0),
            dst_ref=row_of(matrix_at(slabs, at % 2), row),
            send_sem=slab_send.at[at],
            recv_sem=slab_recv.at[at],
            device_id=(around[at], j),
            device_id_type=MESH,
        )
        copy.start()
        slab_copies.append(copy)
    got_inv_xt = send(row_of(invs[0], 0), row_of(ahead_xt, 0), x_up_t_down)
    got_u_xt = send(row_of(links[3], 7), row_of(behind_xt, 7), x_down_t_up)

    got_ut.wait_recv()

    def inv_ahead(nu):
        return load_row(matrix_at(ahead_t, nu), 0)

    got_qt.wait_recv()

    def behind_t(nu):
        return load_row(matrix_at(qt_in, nu), 7)

    for nu in (1, 2):
        n_nt = mm(m_shift(load(links[3]), nu, 1), m_shift(load(invs[nu]), 3, 1, inv_ahead(nu)))
        a_nt = less_inverse(mm(load(links[nu]), mm(n_nt, load(invs[3]))))
        m_nt = mm(load(invs[3]), load(links[nu]))
        lower = mm(m_shift(load(matrix_at(qt, nu)), 3, -1, behind_t(nu)), load(invs[nu]))
        accumulate(nu, sub(a_nt, less_inverse(lower)), 1)
        to_t = sub(m_shift(less_inverse(mm(n_nt, m_nt)), nu, -1), a_nt)
        if nu == 1:
            store(matrix_at(acc, 3), to_t)
        else:
            accumulate(3, to_t, 1)

    for copy in slab_copies:
        copy.wait_recv()
    slot = 2 * t_of
    even, odd = load(matrix_at(slabs, 0)), load(matrix_at(slabs, 1))
    if n_ta - 1 < 2 * ROWS - 1:
        even = unit_where(even, slot >= n_ta - 1)
    odd = unit_where(odd, slot + 1 >= n_ta - 1)
    others = mm(even, odd)
    for step in (1, 2, 4):
        others = mm(others, tuple(pltpu.roll(x, ROWS - step, 2) for x in others))
    others = tuple(jnp.broadcast_to(x[:, :, 0:1, :], x.shape) for x in others)
    line = mm(mm(load(slab), others), load(prefix))
    back = adj(line)
    former = (add_diagonal(FUGACITY * line[0], 1.0), FUGACITY * line[1])
    latter = (add_diagonal(ANTI_FUGACITY * back[0], 1.0), ANTI_FUGACITY * back[1])
    drift = sub(inverse(latter), inverse(former))
    weight = 4.0 * 3.0 / COUPLING
    accumulate(3, (weight * drift[0], weight * drift[1]), 1)

    for nu in (3, 1, 2):
        got_ux[nu].wait_recv()
        halo = inv_ahead(0) if nu == 3 else (None, None)
        n_xn = mm(load(matrix_at(ahead_x, nu - 1)), m_shift(load(invs[0]), nu, 1, halo))
        a_xn = less_inverse(mm(load(links[0]), mm(n_xn, load(invs[nu]))))
        if nu == 3:
            got_u_xt.wait_recv()
            ahead = load_row(behind_xt, 7)
            corner = mm(load(matrix_at(qt, 0)), load(matrix_at(ahead_x, 2)))
            corner = m_shift(corner, 3, -1, mm(behind_t(0), ahead))
            store(matrix_at(acc, 0), sub(a_xn, less_inverse(mm(corner, load(invs[0])))))
        else:
            m_xn = mm(load(invs[nu]), load(links[0]))
            lower = m_shift(less_inverse(mm(m_xn, n_xn)), nu, -1)
            accumulate(0, sub(a_xn, lower), 1)
        got_qx[nu].wait_recv()
        corner = load(matrix_at(qx_in, nu - 1))
        if nu == 3:
            got_inv_xt.wait_recv()
            ahead = load_row(ahead_xt, 0)
            fixed = mm(ahead, corner)
            corner = tuple(jnp.where(t_of == ROWS - 1, b, a) for a, b in zip(corner, fixed))
        accumulate(nu, sub(less_inverse(mm(load(links[nu]), corner)), a_xn), 1)

    loads[4].wait()
    c = math.sqrt(STEP_SIZE)

    def update(d):
        x = load(matrix_at(acc, d))
        w = -STEP_SIZE * COUPLING / 3.0
        mean_r = (x[0][0, 0] + x[0][1, 1] + x[0][2, 2]) * (1.0 / 3.0)
        mean_i = (x[1][0, 0] + x[1][1, 1] + x[1][2, 2]) * (1.0 / 3.0)
        n = [c * noise[d, a] for a in range(8)]
        n7 = n[7] * (1.0 / math.sqrt(3.0))
        real = {(0, 1): n[1], (0, 2): n[4], (1, 2): n[6]}
        imag = {(0, 1): n[0], (0, 2): n[3], (1, 2): n[5]}
        diag = (n[2] + n7, n7 - n[2], -2.0 * n7)
        yr, yi = [], []
        for a in range(3):
            row_r, row_i = [], []
            for b in range(3):
                if a == b:
                    row_r.append(w * (x[0][a, b] - mean_r))
                    row_i.append(w * (x[1][a, b] - mean_i) + diag[a])
                elif a < b:
                    row_r.append(w * x[0][a, b] + real[a, b])
                    row_i.append(w * x[1][a, b] + imag[a, b])
                else:
                    row_r.append(w * x[0][a, b] - real[b, a])
                    row_i.append(w * x[1][a, b] + imag[b, a])
            yr.append(jnp.stack(row_r))
            yi.append(jnp.stack(row_i))
        return exp_times((jnp.stack(yr), jnp.stack(yi)), load(links[d]))


    def exchange(step, link):
        m = link(0)
        plus = gram_rows(m)
        herm_at(gx, step)[...] = h_pack(gram_cols(m))
        got = [send(herm_at(gx, step), herm_at(gx_in, step), x_up)]
        got.append(send(row_of(herm_at(gx, step), 0), row_of(herm_at(gx_in, 2 + step), 0), x_up_t_down))
        m = link(3)
        plus = h_add(plus, gram_rows(m))
        columns = h_pack(gram_cols(m))
        herm_at(gt, step)[...] = columns
        got.append(send(row_of(herm_at(gt, step), 7), row_of(herm_at(gt_in, step), 7), t_up))
        got.append(send(row_of(herm_at(gt, step), 7), row_of(herm_at(gt_in, 2 + step), 7), x_down_t_up))
        minus = jnp.where(index_of(0, 3) == 0, 0.0, pltpu.roll(columns, 1, 1))
        for d in (1, 2):
            m = link(d)
            plus = h_add(plus, gram_rows(m))
            minus = minus + shift(h_pack(gram_cols(m)), d, -1)
        herm_at(part, step)[...] = h_pack(plus) - minus
        got.append(send(herm_at(part, step), herm_at(part_in, step), x_down))
        got.append(send(row_of(herm_at(part, step), 0), row_of(herm_at(part_in, 2 + step), 0), t_down))
        return plus[0][0] + plus[0][1] + plus[0][2], got

    def transforms(step, got):
        for copy in got:
            copy.wait_recv()
        first = index_of(0, 3) == 0
        here = herm_at(part, step)[...] - herm_at(gx_in, step)[...] - jnp.where(first, herm_at(gt_in, step)[:, 7:8, :], 0.0)
        low, high = cooling_pair(h_unpack(here))
        next_t = herm_at(part_in, 2 + step)[:, 0:1, :] - herm_at(gx_in, 2 + step)[:, 0:1, :] - herm_at(gt, step)[:, 7:8, :]
        next_t = h_pack(cooling_pair(h_unpack(next_t))[1])
        high_t = h_unpack(shift(h_pack(high), 3, 1, next_t))
        next_x = herm_at(part_in, step)[...] - herm_at(gx, step)[...] - jnp.where(first, herm_at(gt_in, 2 + step)[:, 7:8, :], 0.0)
        high_x = cooling_pair(h_unpack(next_x))[1]
        return low, (high_x, h_shift(high, 1, 1), h_shift(high, 2, 1), high_t)

    def first_links(d):
        m = update(d)
        store(matrix_at(new, d), m)
        return m

    norm, got = exchange(0, first_links)
    norms = [norm]
    low, high = transforms(0, got)

    def second_links(d):
        m = times_h(h_times(low, load(matrix_at(new, d))), high[d])
        store(matrix_at(new, d), m)
        return m

    norm, got = exchange(1, second_links)
    norms.append(norm)
    low, high = transforms(1, got)

    total = None
    for d in range(4):
        m = times_h(h_times(low, load(matrix_at(new, d))), high[d])
        store(matrix_at(out, d), m)
        squares = m[0] * m[0] + m[1] * m[1]
        squares = squares[0] + squares[1] + squares[2]
        squares = squares[0] + squares[1] + squares[2]
        total = squares if total is None else total + squares
    norms.append(total)


    row, lane = index_of(0, 2), index_of(1, 2)
    spread = jnp.zeros(TILE, jnp.float32)
    for at, value in enumerate(norms):
        sums = jnp.sum(value, axis=1, keepdims=True)
        spread = jnp.where(lane == row + ROWS * at, sums, spread)
    mine = jnp.sum(spread, axis=0, keepdims=True)
    norm_row[0:1, :] = mine
    norm_rows[j, 0:1, :] = mine

    def norm_copy(d, at):
        return pltpu.make_async_remote_copy(
            src_ref=norm_row.at[0:1, :],
            dst_ref=norm_rows.at[at, 0:1, :],
            send_sem=norm_send.at[d],
            recv_sem=norm_recv.at[at],
            device_id=(k, group[d]),
            device_id_type=MESH,
        )

    norm_copies = [norm_copy(d, j) for d in range(n_sa - 1)]
    for copy in norm_copies:
        copy.start()
    for copy in started + slab_copies:
        copy.wait_send()
    for d in range(n_sa - 1):
        norm_copy(d, group[d]).wait_recv()
    total = norm_rows[0, 0:1, :]
    for at in range(1, n_sa):
        total = total + norm_rows[at, 0:1, :]
    total = total * (1.0 / (4.0 * n_sa * LANES)) - 3.0
    for at in range(3):
        norm_ref[at : at + 1, :] = total[:, ROWS * at : ROWS * (at + 1)]
    for copy in norm_copies:
        copy.wait_send()


def local(gauge_links, noise_field):
    n_ta, n_sa = lax.axis_size("ta"), lax.axis_size("sa")
    n_in = max(n_sa // 4, 2)
    shape = (4 * MAT,) + TILE
    vmem = lambda *s: pltpu.VMEM(s, jnp.float32)
    dma = lambda n: pltpu.SemaphoreType.DMA((n,))
    cooled, norms = pl.pallas_call(
        functools.partial(kernel, (n_ta, n_sa, n_in)),
        out_shape=(
            pltpu.VMEM(shape, jnp.float32),
            pltpu.VMEM((3, ROWS), jnp.float32),
        ),
        in_specs=[pl.BlockSpec(memory_space=pltpu.HBM)] * 2,
        out_specs=(pl.BlockSpec(memory_space=pltpu.VMEM),) * 2,
        scratch_shapes=[
            vmem(*shape),
            vmem(4, 8, *TILE),
            vmem(*shape),
            vmem(3 * MAT, *TILE),
            vmem(3 * MAT, *TILE),
            vmem(MAT, *TILE),
            vmem(MAT, *TILE),
            vmem(3 * MAT, *TILE),
            vmem(3 * MAT, *TILE),
            vmem(3 * MAT, *TILE),
            vmem(3 * MAT, *TILE),
            vmem(MAT, *TILE),
            vmem(2 * MAT, *TILE),
            vmem(MAT, *TILE),
            vmem(*shape),
            vmem(*shape),
            vmem(2 * HERM, *TILE),
            vmem(4 * HERM, *TILE),
            vmem(2 * HERM, *TILE),
            vmem(4 * HERM, *TILE),
            vmem(2 * HERM, *TILE),
            vmem(4 * HERM, *TILE),
            vmem(*TILE),
            vmem(n_sa, *TILE),
            dma(5),
            dma(22),
            dma(22),
            dma(n_ta - 1),
            dma(n_ta - 1),
            dma(n_sa - 1),
            dma(n_sa),
        ],
        compiler_params=pltpu.CompilerParams(
            collective_id=0, has_side_effects=True, vmem_limit_bytes=VMEM_LIMIT
        ),
        name="langevin_step",
    )(
        pltpu.with_memory_space_constraint(gauge_links.reshape(shape), pltpu.HBM),
        pltpu.with_memory_space_constraint(noise_field.reshape((4, 8) + TILE), pltpu.HBM),
    )
    return cooled.reshape(gauge_links.shape), norms


def solution(mesh):
    placed = (P(None, None, None, None, "sa", "ta", None), P(None, None, "sa", "ta", None))
    return jax.shard_map(
        local,
        mesh=mesh,
        in_specs=placed,
        out_specs=(P(None, None, None, None, "sa", "ta", None), P(None, "ta")),
        check_vma=False,
    )
```

time: 46.7 us -> 41.1 us (0.88)
  the two profiles are of different devices: /device:TPU:2 before, /device:TPU:1 now
where the time goes in v1:
time: 41.1 us; the launch traced here: 40.9 us
  Pallas kernels  39 us (95%)
  local copies, waits for them, and re-layouts  1.29 us (3%)
  between operations  0.64 us (2%)
    pallas_call x1, Pallas kernels, local(): pl.pallas_call(functools.partial(kernel, (n_ta, n_sa, n_in)), out_shape=(...  39 us
    unnamed x2, local copies, waits for them, and re-layouts  1.29 us

profile of v1, /device:TPU:1, one launch (start us, length us, event | category | flops | bytes accessed | tf_op | source)
XLA Modules:
  0.0 40.9 jit_solution(9739045651499700671)
XLA Ops:
  0.6 39.0 %langevin_step.1 = (f32[72,8,128]{2,1,0:T(8,128)S(1)}, f32[3,8]{1,0:T(4,128)S(1)}) custom-call(f32[72,8,128]{2,1,0:T(8,128)} %bitcast.6, f32[4,8,8,128]{3,2,1,0:T(8,128)} %bitcast.7), custom_call_target="tpu_custom_call" | custom-call | tf_op jit(solution)/shard_map/langevin_step/pallas_call | solution.py:673
  39.6 0.7 %copy.7 = f32[4,2,3,3,1,8,128]{6,5,4,3,2,1,0:T(8,128)} copy(f32[4,2,3,3,1,8,128]{6,5,4,3,2,1,0:T(8,128)S(1)} %bitcast.5) | data formatting | bytes 589824
  40.3 0.6 %copy.8 = f32[3,8]{1,0:T(4,128)} copy(f32[3,8]{1,0:T(4,128)S(1)} %get-tuple-element.9) | data formatting | bytes 192

commit v2 on v1

--- a/solution.py
+++ b/solution.py
@@ -342,6 +342,7 @@
     slab,
     slabs,
     prefix,
+    middles,
     acc,
     new,
     gx,
@@ -379,7 +380,7 @@
         (min(a, n_out - a) + min(b, n_in - b), (k, at))
         for (a, b), at in zip(far_first(n_out, n_in), group)
     ]
-    partners += [(min(d, n_ta - d) / 2, (at, j)) for d, at in enumerate(around, 1)]
+    partners += [(8 + min(d, n_ta - d), (at, j)) for d, at in enumerate(around, 1)]
     partners += [(2.5, x_up_t_down), (2.5, x_down_t_up)]
     partners = [device for _, device in sorted(partners, key=lambda p: -p[0])]
     for device in partners:
@@ -420,6 +421,7 @@
 
     for nu in (1, 2):
         middle = mm(load(invs[nu]), load(links[0]))
+        store(matrix_at(middles, nu - 1), middle)
         store(matrix_at(qx, nu - 1), mm(m_shift(load(invs[0]), nu, 1), middle))
     middle = mm(load(invs[3]), load(links[0]))
     store(matrix_at(qt, 0), middle)
@@ -428,7 +430,9 @@
     store(matrix_at(qx, 2), tuple(jnp.where(t_of == ROWS - 1, b, a) for a, b in zip(whole, middle)))
 
     for nu in (1, 2):
-        store(matrix_at(qt, nu), mm(mm(load(invs[3]), load(links[nu])), m_shift(load(links[3]), nu, 1)))
+        middle = mm(load(invs[3]), load(links[nu]))
+        store(matrix_at(middles, 1 + nu), middle)
+        store(matrix_at(qt, nu), mm(middle, m_shift(load(links[3]), nu, 1)))
 
     store(slab, time_scan(load(links[3]), True))
     scan = time_scan(load(links[3]), False)
@@ -481,7 +485,7 @@
     for nu in (1, 2):
         n_nt = mm(m_shift(load(links[3]), nu, 1), m_shift(load(invs[nu]), 3, 1, inv_ahead(nu)))
         a_nt = less_inverse(mm(load(links[nu]), mm(n_nt, load(invs[3]))))
-        m_nt = mm(load(invs[3]), load(links[nu]))
+        m_nt = load(matrix_at(middles, 1 + nu))
         lower = mm(m_shift(load(matrix_at(qt, nu)), 3, -1, behind_t(nu)), load(invs[nu]))
         accumulate(nu, sub(a_nt, less_inverse(lower)), 1)
         to_t = sub(m_shift(less_inverse(mm(n_nt, m_nt)), nu, -1), a_nt)
@@ -521,7 +525,7 @@
             corner = m_shift(corner, 3, -1, mm(behind_t(0), ahead))
             store(matrix_at(acc, 0), sub(a_xn, less_inverse(mm(corner, load(invs[0])))))
         else:
-            m_xn = mm(load(invs[nu]), load(links[0]))
+            m_xn = load(matrix_at(middles, nu - 1))
             lower = m_shift(less_inverse(mm(m_xn, n_xn)), nu, -1)
             accumulate(0, sub(a_xn, lower), 1)
         got_qx[nu].wait_recv()
@@ -564,74 +568,101 @@
         return exp_times((jnp.stack(yr), jnp.stack(yi)), load(links[d]))
 
 
-    def exchange(step, link):
-        m = link(0)
-        plus = gram_rows(m)
-        herm_at(gx, step)[...] = h_pack(gram_cols(m))
-        got = [send(herm_at(gx, step), herm_at(gx_in, step), x_up)]
-        got.append(send(row_of(herm_at(gx, step), 0), row_of(herm_at(gx_in, 2 + step), 0), x_up_t_down))
-        m = link(3)
-        plus = h_add(plus, gram_rows(m))
-        columns = h_pack(gram_cols(m))
-        herm_at(gt, step)[...] = columns
-        got.append(send(row_of(herm_at(gt, step), 7), row_of(herm_at(gt_in, step), 7), t_up))
-        got.append(send(row_of(herm_at(gt, step), 7), row_of(herm_at(gt_in, 2 + step), 7), x_down_t_up))
-        minus = jnp.where(index_of(0, 3) == 0, 0.0, pltpu.roll(columns, 1, 1))
-        for d in (1, 2):
+    def exchange(step, link, order):
+        plus = minus = None
+        got = {}
+        for d in order:
             m = link(d)
-            plus = h_add(plus, gram_rows(m))
-            minus = minus + shift(h_pack(gram_cols(m)), d, -1)
-        herm_at(part, step)[...] = h_pack(plus) - minus
-        got.append(send(herm_at(part, step), herm_at(part_in, step), x_down))
-        got.append(send(row_of(herm_at(part, step), 0), row_of(herm_at(part_in, 2 + step), 0), t_down))
+            rows, columns = gram_rows(m), h_pack(gram_cols(m))
+            plus = rows if plus is None else h_add(plus, rows)
+            if d == 0:
+                mine = herm_at(gx, step)
+                mine[...] = columns
+                got["x"] = send(mine, herm_at(gx_in, step), x_up)
+                there = row_of(herm_at(gx_in, 2 + step), 0)
+                got["x ahead"] = send(row_of(mine, 0), there, x_up_t_down)
+                continue
+            if d == 3:
+                mine = herm_at(gt, step)
+                mine[...] = columns
+                mine = row_of(mine, 7)
+                got["t"] = send(mine, row_of(herm_at(gt_in, step), 7), t_up)
+                got["t ahead"] = send(mine, row_of(herm_at(gt_in, 2 + step), 7), x_down_t_up)
+                lagged = jnp.where(index_of(0, 3) == 0, 0.0, pltpu.roll(columns, 1, 1))
+            else:
+                lagged = shift(columns, d, -1)
+            minus = lagged if minus is None else minus + lagged
+        mine = herm_at(part, step)
+        mine[...] = h_pack(plus) - minus
+        got["part x"] = send(mine, herm_at(part_in, step), x_down)
+        got["part t"] = send(row_of(mine, 0), row_of(herm_at(part_in, 2 + step), 0), t_down)
         return plus[0][0] + plus[0][1] + plus[0][2], got
 
     def transforms(step, got):
-        for copy in got:
-            copy.wait_recv()
         first = index_of(0, 3) == 0
-        here = herm_at(part, step)[...] - herm_at(gx_in, step)[...] - jnp.where(first, herm_at(gt_in, step)[:, 7:8, :], 0.0)
+        got["t"].wait_recv()
+        got["x"].wait_recv()
+        lag = jnp.where(first, herm_at(gt_in, step)[:, 7:8, :], 0.0)
+        here = herm_at(part, step)[...] - herm_at(gx_in, step)[...] - lag
         low, high = cooling_pair(h_unpack(here))
-        next_t = herm_at(part_in, 2 + step)[:, 0:1, :] - herm_at(gx_in, 2 + step)[:, 0:1, :] - herm_at(gt, step)[:, 7:8, :]
-        next_t = h_pack(cooling_pair(h_unpack(next_t))[1])
-        high_t = h_unpack(shift(h_pack(high), 3, 1, next_t))
-        next_x = herm_at(part_in, step)[...] - herm_at(gx, step)[...] - jnp.where(first, herm_at(gt_in, 2 + step)[:, 7:8, :], 0.0)
-        high_x = cooling_pair(h_unpack(next_x))[1]
-        return low, (high_x, h_shift(high, 1, 1), h_shift(high, 2, 1), high_t)
+
+        def ahead(d):
+            if d == 3:
+                got["part t"].wait_recv()
+                got["x ahead"].wait_recv()
+                g = herm_at(part_in, 2 + step)[:, 0:1, :] - herm_at(gx_in, 2 + step)[:, 0:1, :]
+                g = g - herm_at(gt, step)[:, 7:8, :]
+                halo = h_pack(cooling_pair(h_unpack(g))[1])
+                return h_unpack(shift(h_pack(high), 3, 1, halo))
+            if d == 0:
+                got["t ahead"].wait_recv()
+                got["part x"].wait_recv()
+                g = herm_at(part_in, step)[...] - herm_at(gx, step)[...]
+                g = g - jnp.where(first, herm_at(gt_in, 2 + step)[:, 7:8, :], 0.0)
+                return cooling_pair(h_unpack(g))[1]
+            return h_shift(high, d, 1)
+
+        return low, ahead
+
+    def lane_sums(value):
+        return jnp.sum(value, axis=1, keepdims=True)
 
     def first_links(d):
         m = update(d)
         store(matrix_at(new, d), m)
         return m
 
-    norm, got = exchange(0, first_links)
-    norms = [norm]
-    low, high = transforms(0, got)
+    norm, got = exchange(0, first_links, (0, 3, 1, 2))
+    norms = [lane_sums(norm)]
+    low, ahead = transforms(0, got)
+
+    def cooled_link(d):
+        m = h_times(low, load(matrix_at(new, d)))
+        return times_h(m, ahead(d))
 
     def second_links(d):
-        m = times_h(h_times(low, load(matrix_at(new, d))), high[d])
+        m = cooled_link(d)
         store(matrix_at(new, d), m)
         return m
 
-    norm, got = exchange(1, second_links)
-    norms.append(norm)
-    low, high = transforms(1, got)
+    norm, got = exchange(1, second_links, (1, 2, 3, 0))
+    norms.append(lane_sums(norm))
+    low, ahead = transforms(1, got)
 
     total = None
-    for d in range(4):
-        m = times_h(h_times(low, load(matrix_at(new, d))), high[d])
+    for d in (1, 2, 3, 0):
+        m = cooled_link(d)
         store(matrix_at(out, d), m)
         squares = m[0] * m[0] + m[1] * m[1]
         squares = squares[0] + squares[1] + squares[2]
         squares = squares[0] + squares[1] + squares[2]
         total = squares if total is None else total + squares
-    norms.append(total)
+    norms.append(lane_sums(total))
 
 
     row, lane = index_of(0, 2), index_of(1, 2)
     spread = jnp.zeros(TILE, jnp.float32)
-    for at, value in enumerate(norms):
-        sums = jnp.sum(value, axis=1, keepdims=True)
+    for at, sums in enumerate(norms):
         spread = jnp.where(lane == row + ROWS * at, sums, spread)
     mine = jnp.sum(spread, axis=0, keepdims=True)
     norm_row[0:1, :] = mine
@@ -662,6 +693,17 @@
         norm_ref[at : at + 1, :] = total[:, ROWS * at : ROWS * (at + 1)]
     for copy in norm_copies:
         copy.wait_send()
+
+
+def finish(links, norms, links_out, norms_out, sem):
+    copies = (
+        pltpu.make_async_copy(links, links_out, sem.at[0]),
+        pltpu.make_async_copy(norms, norms_out, sem.at[1]),
+    )
+    for copy in copies:
+        copy.start()
+    for copy in copies:
+        copy.wait()
 
 
 def local(gauge_links, noise_field):
@@ -693,6 +735,7 @@
             vmem(MAT, *TILE),
             vmem(2 * MAT, *TILE),
             vmem(MAT, *TILE),
+            vmem(4 * MAT, *TILE),
             vmem(*shape),
             vmem(*shape),
             vmem(2 * HERM, *TILE),
@@ -719,6 +762,18 @@
         pltpu.with_memory_space_constraint(gauge_links.reshape(shape), pltpu.HBM),
         pltpu.with_memory_space_constraint(noise_field.reshape((4, 8) + TILE), pltpu.HBM),
     )
+    cooled, norms = pl.pallas_call(
+        finish,
+        out_shape=(
+            jax.ShapeDtypeStruct(shape, jnp.float32),
+            jax.ShapeDtypeStruct((3, ROWS), jnp.float32),
+        ),
+        in_specs=[pl.BlockSpec(memory_space=pltpu.VMEM)] * 2,
+        out_specs=(pl.BlockSpec(memory_space=pltpu.HBM),) * 2,
+        scratch_shapes=[dma(2)],
+        compiler_params=pltpu.CompilerParams(vmem_limit_bytes=VMEM_LIMIT),
+        name="write_out",
+    )(cooled, norms)
     return cooled.reshape(gauge_links.shape), norms
 
 

time: 41.1 us -> 39.5 us (0.961)
  local copies, waits for them, and re-layouts: 1.29 us -> 0 us
  Pallas kernels: 39 us -> 38.5 us
    unnamed x2 -> x0, local copies, waits for them, and re-layouts: 1.29 us -> none
    pallas_call x1, Pallas kernels: 39 us -> 37.7 us  [local(): pl.pallas_call(functools.partial(kernel, (n_ta, n_sa, n_in)), out_shape=(...]
    pallas_call x0 -> x1, Pallas kernels: none -> 0.74 us  [local(): pl.pallas_call(finish, out_shape=(jax.ShapeDtypeStruct(shape, jnp.float32...]
where the time goes in v2:
time: 39.5 us; the launch traced here: 39.1 us
  Pallas kernels  38.5 us (97%)
  between operations  0.64 us (2%)
    pallas_call x1, Pallas kernels, local(): pl.pallas_call(functools.partial(kernel, (n_ta, n_sa, n_in)), out_shape=(...  37.7 us

profile of v2, /device:TPU:1, one launch (start us, length us, event | category | flops | bytes accessed | tf_op | source)
XLA Modules:
  0.0 39.1 jit_solution(7847648844057683368)
XLA Ops:
  0.6 37.7 %langevin_step.1 = (f32[72,8,128]{2,1,0:T(8,128)S(1)}, f32[3,8]{1,0:T(4,128)S(1)}) custom-call(f32[72,8,128]{2,1,0:T(8,128)} %bitcast.5, f32[4,8,8,128]{3,2,1,0:T(8,128)} %bitcast.6), custom_call_target="tpu_custom_call" | custom-call | tf_op jit(solution)/shard_map/langevin_step/pallas_call | solution.py:715
  38.4 0.7 %write_out.1 = (f32[72,8,128]{2,1,0:T(8,128)}, f32[3,8]{1,0:T(4,128)}) custom-call(f32[72,8,128]{2,1,0:T(8,128)S(1)} %get-tuple-element.6.links, f32[3,8]{1,0:T(4,128)S(1)} %get-tuple-element.7.norms), custom_call_target="tpu_custom_call" | custom-call | tf_op jit(solution)/shard_map/write_out/pallas_call | solution.py:765

commit v3 on v2

--- a/solution.py
+++ b/solution.py
@@ -383,13 +383,16 @@
     partners += [(8 + min(d, n_ta - d), (at, j)) for d, at in enumerate(around, 1)]
     partners += [(2.5, x_up_t_down), (2.5, x_down_t_up)]
     partners = [device for _, device in sorted(partners, key=lambda p: -p[0])]
-    for device in partners:
-        pl.semaphore_signal(barrier, inc=1, device_id=device, device_id_type=MESH)
-
+    def greet(devices):
+        for device in devices:
+            pl.semaphore_signal(barrier, inc=1, device_id=device, device_id_type=MESH)
+
+    greet(partners[: n_ta - 1])
     loads = [pltpu.make_async_copy(matrix_at(u_hbm, d), matrix_at(u, d), local_sem.at[d]) for d in range(4)]
     loads.append(pltpu.make_async_copy(noise_hbm, noise, local_sem.at[4]))
     for copy in loads:
         copy.start()
+    greet(partners[n_ta - 1 :])
 
     started = []
 
@@ -435,23 +438,18 @@
         store(matrix_at(qt, nu), mm(middle, m_shift(load(links[3]), nu, 1)))
 
     store(slab, time_scan(load(links[3]), True))
-    scan = time_scan(load(links[3]), False)
-    store(prefix, unit_where(tuple(pltpu.roll(x, 1, 2) for x in scan), t_of == 0))
-
-    u_1, u_2 = load(links[1]), load(links[2])
-    n_12 = mm(m_shift(u_2, 1, 1), m_shift(load(invs[1]), 2, 1))
-    m_12 = mm(load(invs[2]), u_1)
-    a_12 = less_inverse(mm(u_1, mm(n_12, load(invs[2]))))
-    store(matrix_at(acc, 1), sub(a_12, m_shift(less_inverse(mm(m_12, n_12)), 2, -1)))
-    store(matrix_at(acc, 2), sub(m_shift(less_inverse(mm(n_12, m_12)), 1, -1), a_12))
 
 
     pl.semaphore_wait(barrier, len(partners))
 
     got_ux, got_qx = {}, {}
-    for nu in (3, 1, 2):
+
+    def send_x(nu):
         got_ux[nu] = send(links[nu], matrix_at(ahead_x, nu - 1), x_down)
         got_qx[nu] = send(matrix_at(qx, nu - 1), matrix_at(qx_in, nu - 1), x_up)
+
+    send_x(3)
+    send_x(1)
     got_ut = send(inv.at[0 : 3 * MAT, 0:1, :], row_of(ahead_t, 0), t_down)
     got_qt = send(row_of(qt, 7), row_of(qt_in, 7), t_up)
     slab_copies = []
@@ -472,6 +470,19 @@
     got_inv_xt = send(row_of(invs[0], 0), row_of(ahead_xt, 0), x_up_t_down)
     got_u_xt = send(row_of(links[3], 7), row_of(behind_xt, 7), x_down_t_up)
 
+
+    scan = time_scan(load(links[3]), False)
+    store(prefix, unit_where(tuple(pltpu.roll(x, 1, 2) for x in scan), t_of == 0))
+
+    u_1, u_2 = load(links[1]), load(links[2])
+    n_12 = mm(m_shift(u_2, 1, 1), m_shift(load(invs[1]), 2, 1))
+    m_12 = mm(load(invs[2]), u_1)
+    a_12 = less_inverse(mm(u_1, mm(n_12, load(invs[2]))))
+    store(matrix_at(acc, 1), sub(a_12, m_shift(less_inverse(mm(m_12, n_12)), 2, -1)))
+    store(matrix_at(acc, 2), sub(m_shift(less_inverse(mm(n_12, m_12)), 1, -1), a_12))
+
+    send_x(2)
+
     got_ut.wait_recv()
 
     def inv_ahead(nu):
@@ -513,7 +524,7 @@
     weight = 4.0 * 3.0 / COUPLING
     accumulate(3, (weight * drift[0], weight * drift[1]), 1)
 
-    for nu in (3, 1, 2):
+    def x_plane(nu):
         got_ux[nu].wait_recv()
         halo = inv_ahead(0) if nu == 3 else (None, None)
         n_xn = mm(load(matrix_at(ahead_x, nu - 1)), m_shift(load(invs[0]), nu, 1, halo))
@@ -536,6 +547,9 @@
             fixed = mm(ahead, corner)
             corner = tuple(jnp.where(t_of == ROWS - 1, b, a) for a, b in zip(corner, fixed))
         accumulate(nu, sub(less_inverse(mm(load(links[nu]), corner)), a_xn), 1)
+
+    x_plane(3)
+    x_plane(1)
 
     loads[4].wait()
     c = math.sqrt(STEP_SIZE)
@@ -628,11 +642,13 @@
         return jnp.sum(value, axis=1, keepdims=True)
 
     def first_links(d):
+        if d == 0:
+            x_plane(2)
         m = update(d)
         store(matrix_at(new, d), m)
         return m
 
-    norm, got = exchange(0, first_links, (0, 3, 1, 2))
+    norm, got = exchange(0, first_links, (3, 1, 0, 2))
     norms = [lane_sums(norm)]
     low, ahead = transforms(0, got)
 

time: 39.5 us -> 39 us (0.987)
  Pallas kernels: 38.5 us -> 38 us
    pallas_call x1, Pallas kernels: 37.7 us -> 37.3 us  [local(): pl.pallas_call(functools.partial(kernel, (n_ta, n_sa, n_in)), out_shape=(...]
where the time goes in v3:
time: 39 us; the launch traced here: 38.7 us
  Pallas kernels  38 us (97%)
  between operations  0.64 us (2%)
    pallas_call x1, Pallas kernels, local(): pl.pallas_call(functools.partial(kernel, (n_ta, n_sa, n_in)), out_shape=(...  37.3 us

profile of v3, /device:TPU:1, one launch (start us, length us, event | category | flops | bytes accessed | tf_op | source)
XLA Modules:
  0.0 38.7 jit_solution(5292450960819060724)
XLA Ops:
  0.6 37.3 %langevin_step.1 = (f32[72,8,128]{2,1,0:T(8,128)S(1)}, f32[3,8]{1,0:T(4,128)S(1)}) custom-call(f32[72,8,128]{2,1,0:T(8,128)} %bitcast.5, f32[4,8,8,128]{3,2,1,0:T(8,128)} %bitcast.6), custom_call_target="tpu_custom_call" | custom-call | tf_op jit(solution)/shard_map/langevin_step/pallas_call | solution.py:731
  37.9 0.7 %write_out.1 = (f32[72,8,128]{2,1,0:T(8,128)}, f32[3,8]{1,0:T(4,128)}) custom-call(f32[72,8,128]{2,1,0:T(8,128)S(1)} %get-tuple-element.6.links, f32[3,8]{1,0:T(4,128)S(1)} %get-tuple-element.7.norms), custom_call_target="tpu_custom_call" | custom-call | tf_op jit(solution)/shard_map/write_out/pallas_call | solution.py:781
